TPU v7x, 32 devices: a whole 2x2x4 slice. The times are simulated.
32 devices in a mesh: ctx: 4 (over y, core), exp: 8 (over z, x).
Axes of the slice: x: 2, y: 2, z: 4, core: 2. Of those that a mesh axis runs over, the one named last changes fastest.
Arguments:
- mixer_input: bfloat16 [512, 2, 8192], P('ctx', None, 'exp'), may hold values from -6 to 6
- gate_in: bfloat16 [512, 2, 8192], P('ctx', None, 'exp'), may hold values from -6 to 6
- step_size: float32 [512, 2, 8192], P('ctx', None, 'exp'), may hold values from 0.004 to 10
- decay_rate: float32 [16, 8192], P(None, 'exp'), may hold values from 0.03 to 2.5
- state_in: float32 [512, 2, 16], P('ctx'), may hold values from -6 to 6
- state_out: float32 [512, 2, 16], P('ctx'), may hold values from -6 to 6
- skip: float32 [8192], P('exp'), may hold values from 0.5 to 1.5
- out_proj: bfloat16 [8192, 4096], P('exp', 'ctx'), may hold values from -0.0625 to 0.0625
- hidden_in: bfloat16 [512, 2, 4096], P('ctx', None, 'exp'), may hold values from -14 to 14
- norm_gain: float32 [4096], replicated, may hold values from 0.4 to 2.5
- w_gate: bfloat16 [8, 4096, 7168], P('exp', None, 'ctx'), may hold values from -0.09375 to 0.09375
- w_up: bfloat16 [8, 4096, 7168], P('exp', None, 'ctx'), may hold values from -0.09375 to 0.09375
- w_down: bfloat16 [8, 7168, 4096], P('exp', 'ctx'), may hold values from -0.0625 to 0.0625
- route_ids: int32 [512, 2, 2], P('ctx'), may hold values from 0 to 7, all different within a row; in each aligned block of 256 rows (0 to 255, 256 to 511, ..., all dimensions but the last counted through in order) at most 128 rows name the same one
- route_weight: float32 [512, 2, 2], P('ctx'), may hold values from 0.1 to 0.9
Outputs:
- layer_out: bfloat16 [512, 2, 4096], P('ctx', None, 'exp')
Inputs may be any that keep to these rules, and one draw needn't show every extreme that they name: `route_ids`: the 2 experts of a token differ; within the rows of one index of ctx no expert is named by more than 128 rows.
All inputs are finite; a program needn't handle non-finite values.
Results may differ from a plain program's by a relative error of at most 0.009.
Values may be sent and summed in bfloat16 or wider, within the bound.
A program may use at most 256 MiB of HBM per device.

v0:
```python
import functools
import math

import jax
import jax.numpy as jnp
from jax import lax
from jax.experimental import pallas as pl
from jax.experimental.pallas import tpu as pltpu
from jax.sharding import PartitionSpec as P

epsilon = 1e-06
f32, bf16 = jnp.float32, jnp.bfloat16
MESH = pl.DeviceIdType.MESH
VMEM_LIMIT = 48 * 1024 * 1024
HBM = pl.BlockSpec(memory_space=pl.ANY)
SMEM = pl.BlockSpec(memory_space=pltpu.SMEM)
LOCAL = pl.BlockSpec(memory_space=pltpu.VMEM)


def factors(count):
    inner = 2 ** (count.bit_length() // 2 - (1 if count.bit_length() % 2 == 0 else 0))
    return count // inner, inner


def ends_kernel(length, prompts, states, step_ref, signal_ref, rate_ref, into_ref, end_ref):
    tile = step_ref.shape[1:]
    for b in range(prompts):

        def chunk(i, carry):
            held, total = carry
            for u in range(4):
                row = (i * 4 + u) * prompts + b
                step = step_ref[row]
                inflow = step * signal_ref[row]
                held = tuple(
                    jnp.exp2(step * rate_ref[n]) * held[n] + inflow * into_ref[row * states + n]
                    for n in range(states)
                )
                total = total + step
            return held, total

        zero = jnp.zeros(tile, f32)
        held, total = lax.fori_loop(0, length // 4, chunk, ((zero,) * states, zero))
        for n in range(states):
            end_ref[b, n] = held[n]
        end_ref[b, states] = total


def scan_kernel(
    length, prompts, states, step_ref, signal_ref, rate_ref, into_ref, outof_ref, enter_ref, out_ref
):
    for b in range(prompts):

        def chunk(i, held):
            for u in range(4):
                row = (i * 4 + u) * prompts + b
                step = step_ref[row]
                inflow = step * signal_ref[row]
                held = tuple(
                    jnp.exp2(step * rate_ref[n]) * held[n] + inflow * into_ref[row * states + n]
                    for n in range(states)
                )
                terms = [held[n] * outof_ref[row * states + n] for n in range(states)]
                while len(terms) > 1:
                    terms = [p + q for p, q in zip(terms[::2], terms[1::2])]
                out_ref[row] = terms[0]
            return held

        lax.fori_loop(0, length // 4, chunk, tuple(enter_ref[b, n] for n in range(states)))


def exchange(x, out_shape, axis, count, member, mine, source, target, ident):
    def kernel(x_ref, o_ref, send_sem, recv_sem, local_sem):
        q = mine(lax.axis_index(axis))
        me = lax.axis_index(axis)
        barrier = pltpu.get_barrier_semaphore()
        for k in range(1, count):
            peer = member(me, lax.rem(q + k, count))
            pl.semaphore_signal(barrier, inc=1, device_id={axis: peer}, device_id_type=MESH)
        pl.semaphore_wait(barrier, count - 1)
        copies = []
        for k in range(1, count):
            r = lax.rem(q + k, count)
            copies.append(
                pltpu.make_async_remote_copy(
                    src_ref=source(x_ref, r),
                    dst_ref=target(o_ref, q),
                    send_sem=send_sem.at[k - 1],
                    recv_sem=recv_sem.at[k - 1],
                    device_id={axis: member(me, r)},
                    device_id_type=MESH,
                )
            )
            copies[-1].start()
        own = pltpu.make_async_copy(source(x_ref, q), target(o_ref, q), local_sem)
        own.start()
        own.wait()
        for copy in copies:
            copy.wait()

    return pl.pallas_call(
        kernel,
        out_shape=jax.ShapeDtypeStruct(out_shape, x.dtype),
        in_specs=[HBM],
        out_specs=HBM,
        scratch_shapes=[
            pltpu.SemaphoreType.DMA((count - 1,)),
            pltpu.SemaphoreType.DMA((count - 1,)),
            pltpu.SemaphoreType.DMA,
        ],
        compiler_params=pltpu.CompilerParams(collective_id=ident, has_side_effects=True),
    )(x)


def gather_ctx(x, out_shape, count, target, ident):
    axis, chips = "ctx", count // 2

    def kernel(x_ref, o_ref, send_sem, recv_sem, local_sem):
        me = lax.axis_index(axis)
        chip, core = me // 2, lax.rem(me, 2)
        twin = chip * 2 + (1 - core)
        barrier = pltpu.get_barrier_semaphore()
        partners = [twin] + [lax.rem(chip + k, chips) * 2 + core for k in range(1, chips)]
        for peer in partners:
            pl.semaphore_signal(barrier, inc=1, device_id={axis: peer}, device_id_type=MESH)
        pl.semaphore_wait(barrier, chips)

        def push(src, owner, slot, peer):
            copy = pltpu.make_async_remote_copy(
                src_ref=src,
                dst_ref=target(o_ref, owner),
                send_sem=send_sem.at[slot],
                recv_sem=recv_sem.at[slot],
                device_id={axis: peer},
                device_id_type=MESH,
            )
            copy.start()
            return copy

        across = [push(x_ref, me, k, partners[k]) for k in range(1, chips)]
        pending = [push(x_ref, me, 0, twin)]
        own = pltpu.make_async_copy(x_ref, target(o_ref, me), local_sem)
        own.start()
        for k in range(1, chips):
            across[k - 1].wait_recv()
            owner = lax.rem(chip + chips - k, chips) * 2 + core
            pending.append(push(target(o_ref, owner), owner, chips - 1 + k, twin))
        own.wait()
        for copy in across:
            copy.wait_send()
        for copy in pending:
            copy.wait()

    slots = 2 * chips - 1
    return pl.pallas_call(
        kernel,
        out_shape=jax.ShapeDtypeStruct(out_shape, x.dtype),
        in_specs=[HBM],
        out_specs=HBM,
        scratch_shapes=[
            pltpu.SemaphoreType.DMA((slots,)),
            pltpu.SemaphoreType.DMA((slots,)),
            pltpu.SemaphoreType.DMA,
        ],
        compiler_params=pltpu.CompilerParams(collective_id=ident, has_side_effects=True),
    )(x)


def block(ref, r):
    return ref.at[r]


def scatter_sum(x, axis, count, ident):
    outer, inner = factors(count) if axis == "exp" else (count // 2, 2)
    rows, columns = x.shape[1:]
    x = x.reshape(outer, inner, rows, columns).transpose(1, 0, 2, 3)
    got = exchange(
        x, x.shape, axis, inner,
        lambda me, r: me // inner * inner + r, lambda me: lax.rem(me, inner),
        block, block, ident,
    )
    part = jnp.sum(got.astype(f32), axis=0).astype(bf16)
    got = exchange(
        part, part.shape, axis, outer,
        lambda me, r: r * inner + lax.rem(me, inner), lambda me: me // inner,
        block, block, ident + 1,
    )
    return jnp.sum(got.astype(f32), axis=0)


def on_device(
    mixer_input,
    gate_in,
    step_size,
    decay_rate,
    state_in,
    state_out,
    skip,
    out_proj,
    hidden_in,
    norm_gain,
    w_gate,
    w_up,
    w_down,
    route_ids,
    route_weight,
):
    slab_len, prompts, channels = mixer_input.shape
    states = decay_rate.shape[0]
    tokens = slab_len * prompts
    n_ctx, n_exp = lax.axis_size("ctx"), lax.axis_size("exp")
    ctx, exp = lax.axis_index("ctx"), lax.axis_index("exp")
    share = hidden_in.shape[-1]
    halves = n_exp // n_ctx
    cap = 4 * tokens // (w_gate.shape[0] * n_exp)

    swap = [
        (c * n_exp + e, (e // halves) * n_exp + c * halves + e % halves)
        for c in range(n_ctx)
        for e in range(n_exp)
    ]
    hidden = lax.ppermute(hidden_in.reshape(tokens, share), ("ctx", "exp"), swap)
    routes = lax.all_gather(route_ids.reshape(tokens, -1), "ctx", axis=0)
    slab = exp // halves

    def selector(routed):
        named = jnp.any(routed[:, :, None] == jnp.arange(n_exp)[None, None, :], axis=1)
        place = jnp.cumsum(named.astype(jnp.int32), axis=0) - 1
        place = jnp.where(named, place, -1).T
        return place[:, None, :] == jnp.arange(cap)[None, :, None]

    lanes = (channels // 128, 128)
    signal = mixer_input.astype(f32).reshape(tokens, *lanes)
    step = step_size.reshape(tokens, *lanes)
    rate = (decay_rate * (-1.0 / math.log(2.0))).reshape(states, *lanes)
    into, outof = state_in.reshape(-1), state_out.reshape(-1)
    plain = pltpu.CompilerParams(vmem_limit_bytes=VMEM_LIMIT)
    ends = pl.pallas_call(
        functools.partial(ends_kernel, slab_len, prompts, states),
        out_shape=jax.ShapeDtypeStruct((prompts, states + 1) + lanes, f32),
        in_specs=[LOCAL, LOCAL, LOCAL, SMEM],
        out_specs=LOCAL,
        compiler_params=plain,
    )(step, signal, rate, into)
    ends = gather_ctx(ends, (n_ctx,) + ends.shape, n_ctx, block, 1)
    entering = jnp.zeros((prompts, states) + lanes, f32)
    for j in range(n_ctx - 1):
        longer = jnp.exp2(ends[j, :, states:] * rate[None]) * entering + ends[j, :, :states]
        entering = jnp.where(j < ctx, longer, entering)
    output = pl.pallas_call(
        functools.partial(scan_kernel, slab_len, prompts, states),
        out_shape=jax.ShapeDtypeStruct((tokens,) + lanes, f32),
        in_specs=[LOCAL, LOCAL, LOCAL, SMEM, SMEM, LOCAL],
        out_specs=LOCAL,
        compiler_params=plain,
    )(step, signal, rate, into, outof, entering)
    output = output.reshape(tokens, channels) + skip * mixer_input.astype(f32).reshape(tokens, -1)
    mixed = (output * jax.nn.silu(gate_in.astype(f32).reshape(tokens, -1))).astype(bf16)

    mixed = gather_ctx(
        mixed, (n_ctx * tokens, channels), n_ctx,
        lambda ref, c: ref.at[pl.ds(pl.multiple_of(c * tokens, tokens), tokens)], 2,
    )
    partial_value = jnp.dot(mixed, out_proj, preferred_element_type=f32).astype(bf16)
    partial_value = partial_value.reshape(n_ctx, tokens, halves, share).transpose(0, 2, 1, 3)
    projected = scatter_sum(partial_value.reshape(n_exp, tokens, share), "exp", n_exp, 3)
    residual = hidden.astype(f32) + projected
    residual_home = lax.ppermute(residual, ("ctx", "exp"), swap)

    chosen = selector(lax.dynamic_index_in_dim(routes, slab, 0, keepdims=False))
    rows = jnp.dot(
        chosen.astype(bf16).reshape(n_exp * cap, tokens),
        residual.astype(bf16),
        preferred_element_type=f32,
    ).astype(bf16)
    whole_axis = (lambda me, r: r, lambda me: me)

    def landing(ref, e):
        s, h = e // halves, lax.rem(e, halves)
        return ref.at[
            pl.ds(pl.multiple_of(s * cap, cap), cap), pl.ds(pl.multiple_of(h * share, share), share)
        ]

    rows = exchange(
        rows.reshape(n_exp, cap, share), (n_ctx * cap, halves * share), "exp", n_exp, *whole_axis,
        block, landing, 5,
    )
    span = halves * share
    rows = gather_ctx(
        rows, (n_ctx * cap, n_ctx * span), n_ctx,
        lambda ref, c: ref.at[:, pl.ds(pl.multiple_of(c * span, span), span)], 6,
    )
    rows = rows.astype(f32)
    scale = lax.rsqrt(jnp.mean(rows * rows, axis=1, keepdims=True) + epsilon)
    segment = (rows * scale * norm_gain).astype(bf16)

    gate_part = jnp.dot(segment, w_gate[0], preferred_element_type=f32)
    up_part = jnp.dot(segment, w_up[0], preferred_element_type=f32)
    activ = (jax.nn.silu(gate_part) * up_part).astype(bf16)
    down = jnp.dot(activ, w_down[0], preferred_element_type=f32).astype(bf16)
    returned = scatter_sum(down.reshape(n_ctx, cap, -1), "ctx", n_ctx, 7)

    own = selector(route_ids.reshape(tokens, -1))
    weights = route_weight.reshape(tokens, -1)
    strength = jnp.sum(jnp.where(route_ids.reshape(tokens, -1) == exp, weights, 0.0), axis=1)
    mine = lax.dynamic_index_in_dim(own, exp, 0, keepdims=False)
    slot_weight = jnp.sum(jnp.where(mine, strength[None, :], 0.0), axis=1)
    contrib = (returned * slot_weight[:, None]).astype(bf16)
    back = exchange(
        contrib, (n_exp, cap, share), "exp", n_exp, *whole_axis,
        lambda ref, e: ref.at[:, pl.ds(pl.multiple_of(e * share, share), share)], block, 9,
    )
    combined = lax.dot_general(
        own.astype(bf16).reshape(n_exp * cap, tokens),
        back.reshape(n_exp * cap, share),
        (((0,), (0,)), ((), ())),
        preferred_element_type=f32,
    )
    return (residual_home + combined).astype(bf16).reshape(slab_len, prompts, share)


def solution(mesh):
    placed = (
        P("ctx", None, "exp"),
        P("ctx", None, "exp"),
        P("ctx", None, "exp"),
        P(None, "exp"),
        P("ctx", None, None),
        P("ctx", None, None),
        P("exp"),
        P("exp", "ctx"),
        P("ctx", None, "exp"),
        P(),
        P("exp", None, "ctx"),
        P("exp", None, "ctx"),
        P("exp", "ctx", None),
        P("ctx", None, None),
        P("ctx", None, None),
    )
    return jax.shard_map(
        on_device, mesh=mesh, in_specs=placed, out_specs=P("ctx", None, "exp"), check_vma=False
    )
```

profile of v0, /device:TPU:11, one launch (start us, length us, event | category | flops | bytes accessed | tf_op | source)
XLA Modules:
  0.0 416.1 jit_solution(15800415801595490867)
XLA Ops:
  1.9 3.6 collective-permute-start
  11.2 5.5 %all_gather.3 = s32[4,256,2]{1,2,0:T(2,128)S(1)} all-gather(s32[1,256,2]{1,2,0:T(2,128)S(1)} %all_gather_reshape.3), channel_id=1, replica_groups=mesh['ctx'=4,'exp'=8] {'ctx'}, dimensions={0}, use_global_device_ids=true | all-gather | bytes 10240 | tf_op jit(solution)/shard_map/all_gather | solution.py:223
  19.5 3.1 reshape.96.step_ref
  23.8 4.6 %shard_map.145.x_ref = f32[2,17,8,128]{3,2,1,0:T(8,128)S(1)} custom-call(f32[256,8,128]{2,1,0:T(8,128)S(1)} %copy-done.2, f32[256,8,128]{2,1,0:T(8,128)S(1)} %reshape.97.signal_ref, f32[16,8,128]{2,1,0:T(8,128)S(1)} %bitcast.88, f32[4096]{0:T(1024)S(1)} %reshape.99.into_ref), custom_call_target="tpu_custom_call" | custom-call | tf_op jit(solution)/shard_map/pallas_call | solution.py:238
  29.1 7.7 %shard_map.146 = f32[4,2,17,8,128]{4,3,2,1,0:T(8,128)} custom-call(f32[2,17,8,128]{3,2,1,0:T(8,128)} %copy-done.4), custom_call_target="tpu_custom_call" | custom-call | tf_op jit(solution)/shard_map/pallas_call | solution.py:155
  42.0 6.4 %shard_map.147 = f32[256,8,128]{2,1,0:T(8,128)S(1)} custom-call(f32[256,8,128]{2,1,0:T(8,128)S(1)} %copy-done.3, f32[256,8,128]{2,1,0:T(8,128)S(1)} %reshape.97.signal_ref, f32[16,8,128]{2,1,0:T(8,128)S(1)} %bitcast.90, f32[4096]{0:T(1024)S(1)} %reshape.99.into_ref, f32[4096]{0:T(1024)S(1)} %reshape.100.outof_ref, f32[2,16,8,128]{3,2,1,0:T(8,128)S(1)} %fusion.23.enter_ref), custom_call_target="tpu_custom_call" | custom-call | tf_op jit(solution)/shard_map/pallas_call | solution.py:250
  48.4 2.8 fusion.21.x_ref
  51.2 17.7 %shard_map.148 = bf16[1024,1024]{1,0:T(8,128)(2,1)} custom-call(bf16[256,1024]{1,0:T(8,128)(2,1)} %fusion.21.x_ref), custom_call_target="tpu_custom_call" | custom-call | tf_op jit(solution)/shard_map/pallas_call | solution.py:155
  69.0 5.2 %convolution_convert_fusion = bf16[1024,1024]{1,0:T(8,128)(2,1)} fusion(bf16[1024,1024]{1,0:T(8,128)(2,1)} %shard_map.148, bf16[1024,1024]{1,0:T(8,128)(2,1)S(1)} %copy-done), kind=kOutput, calls=%fused_computation.18 | convolution fusion | flops 2148532224 | bytes 6291456 | tf_op jit(solution)/shard_map/dot_general | solution.py:264
  74.2 3.3 reshape.105
  79.2 33.1 %shard_map.149 = bf16[2,4,256,512]{3,2,1,0:T(8,128)(2,1)} custom-call(bf16[2,4,256,512]{3,2,1,0:T(8,128)(2,1)} %bitcast.92), custom_call_target="tpu_custom_call" | custom-call | tf_op jit(solution)/shard_map/pallas_call | solution.py:101
  112.3 3.3 reduce_sum.69.x_ref
  115.6 26.0 %shard_map.150 = bf16[4,256,512]{2,1,0:T(8,128)(2,1)} custom-call(bf16[4,256,512]{2,1,0:T(8,128)(2,1)} %reduce_sum.69.x_ref), custom_call_target="tpu_custom_call" | custom-call | tf_op jit(solution)/shard_map/pallas_call | solution.py:101
  146.8 47.5 %shard_map.151.x_ref = bf16[512,1024]{1,0:T(8,128)(2,1)} custom-call(bf16[8,128,512]{2,1,0:T(8,128)(2,1)} %bitcast.93), custom_call_target="tpu_custom_call" | custom-call | tf_op jit(solution)/shard_map/pallas_call | solution.py:101
  194.3 33.1 %shard_map.152 = bf16[512,4096]{1,0:T(8,128)(2,1)} custom-call(bf16[512,1024]{1,0:T(8,128)(2,1)} %shard_map.151.x_ref), custom_call_target="tpu_custom_call" | custom-call | tf_op jit(solution)/shard_map/pallas_call | solution.py:155
  227.4 3.2 fusion.6
  230.8 13.0 %fusion.4 = f32[512,1792]{1,0:T(8,128)} fusion(bf16[1,4096,1792]{2,1,0:T(8,128)(2,1)} %param.25, bf16[512,4096]{1,0:T(8,128)(2,1)S(1)} %copy-done.5, f32[4096]{0:T(1024)S(1)} %copy-done.9, f32[512]{0:T(512)S(1)} %add_rsqrt_fusion), kind=kOutput, calls=%fused_computation.4 | convolution fusion | flops 7524581376 | bytes 22562816 | tf_op jit(solution)/shard_map/dot_general | solution.py:297
  243.8 28.8 %fusion.9 = bf16[512,4096]{1,0:T(8,128)(2,1)} fusion(bf16[1,1792,4096]{2,1,0:T(8,128)(2,1)} %param.27, f32[512,1792]{1,0:T(8,128)} %fusion.4, bf16[1,4096,1792]{2,1,0:T(8,128)(2,1)} %param.26, bf16[512,4096]{1,0:T(8,128)(2,1)} %shard_map.152, f32[4096]{0:T(1024)S(1)} %copy-done.9, f32[512]{0:T(512)S(1)} %add_rsqrt_fusion), kind=kOutput, calls=%fused_computation.11 | convolution fusion | flops 15048376320 | bytes 41437184 | tf_op jit(solution)/shard_map/dot_general | solution.py:300
  272.6 4.6 %copy.52 = bf16[2,2,128,4096]{3,2,0,1:T(8,128)(2,1)} copy(bf16[2,2,128,4096]{3,2,1,0:T(8,128)(2,1)} %bitcast.94) | data formatting | bytes 8388608 | tf_op jit(solution)/shard_map/reshape;reshape | solution.py:176
  277.2 65.3 %shard_map.153 = bf16[2,2,128,4096]{3,2,1,0:T(8,128)(2,1)} custom-call(bf16[2,2,128,4096]{3,2,1,0:T(8,128)(2,1)} %bitcast.91), custom_call_target="tpu_custom_call" | custom-call | tf_op jit(solution)/shard_map/pallas_call | solution.py:101
  342.6 5.0 %reduce_sum.72.x_ref = bf16[2,128,4096]{2,1,0:T(8,128)(2,1)} reduce(bf16[2,2,128,4096]{3,2,1,0:T(8,128)(2,1)} %shard_map.153, bf16[]{:T(256)} %constant.57.clone.1), dimensions={0}, to_apply=%region_9.10 | reduce | flops 1048576 | bytes 6291458 | tf_op jit(solution)/shard_map/reduce_sum | solution.py:182
  347.6 33.6 %shard_map.154 = bf16[2,128,4096]{2,1,0:T(8,128)(2,1)} custom-call(bf16[2,128,4096]{2,1,0:T(8,128)(2,1)} %reduce_sum.72.x_ref), custom_call_target="tpu_custom_call" | custom-call | tf_op jit(solution)/shard_map/pallas_call | solution.py:101
  381.2 2.4 convert_reduce_fusion
  384.8 28.7 %shard_map.155 = bf16[8,128,512]{2,1,0:T(8,128)(2,1)} custom-call(bf16[128,4096]{1,0:T(8,128)(2,1)} %multiply_convert_fusion.1.x_ref), custom_call_target="tpu_custom_call" | custom-call | tf_op jit(solution)/shard_map/pallas_call | solution.py:101
  (69 shorter events, 28.2 us)
Async XLA Ops:
  0.0 69.0 %copy-start = (bf16[1024,1024]{1,0:T(8,128)(2,1)S(1)}, bf16[1024,1024]{1,0:T(8,128)(2,1)}, u32[]{:S(2)}) copy-start(bf16[1024,1024]{1,0:T(8,128)(2,1)} %param.22) | copy-start | bytes 6291460
  0.0 11.1 %copy-start.6 = (f32[16,1024]{1,0:T(8,128)S(1)}, f32[16,1024]{1,0:T(8,128)}, u32[]{:S(2)}) copy-start(f32[16,1024]{1,0:T(8,128)} %param.18) | copy-start | bytes 196612
  0.0 18.6 %copy-start.7 = (f32[128,2,16]{0,2,1:T(8,128)S(1)}, f32[128,2,16]{0,2,1:T(8,128)}, u32[]{:S(2)}) copy-start(f32[128,2,16]{0,2,1:T(8,128)} %param.19) | copy-start | bytes 49156
  0.0 18.9 %copy-start.8 = (f32[128,2,16]{0,2,1:T(8,128)S(1)}, f32[128,2,16]{0,2,1:T(8,128)}, u32[]{:S(2)}) copy-start(f32[128,2,16]{0,2,1:T(8,128)} %param.20) | copy-start | bytes 49156
  1.9 141.5 %collective-permute-start = (bf16[256,512]{1,0:T(8,128)(2,1)}, bf16[256,512]{1,0:T(8,128)(2,1)}, u32[]{:S(2)}, u32[]{:S(2)}) collective-permute-start(bf16[256,512]{1,0:T(8,128)(2,1)} %reshape.95), channel_id=1, source_target_pairs={{0,0},{1,1},{2,8},{3,9},{4,16},{5,17},{6,24},{7,25},{8,2},{9,3},{1... | collective-permute-start | bytes 786440 | tf_op jit(solution)/shard_map/ppermute | solution.py:222
  22.6 1.2 copy-start.2
  28.4 0.7 copy-start.4
  40.8 1.2 copy-start.3
  144.4 270.8 %collective-permute-start.1 = (f32[256,512]{1,0:T(8,128)S(1)}, f32[256,512]{1,0:T(8,128)S(1)}, u32[]{:S(2)}, u32[]{:S(2)}) collective-permute-start(f32[256,512]{1,0:T(8,128)S(1)} %convert_add_fusion), channel_id=1, source_target_pairs={{0,0},{1,1},{2,8},{3,9},{4,16},{5,17},{6,24},{7,25},{8,2},{9,3},{1... | collective-permute-start | bytes 1572872 | tf_op jit(solution)/shard_map/ppermute | solution.py:268
  194.3 36.4 %copy-start.9 = (f32[4096]{0:T(1024)S(1)}, f32[4096]{0:T(1024)}, u32[]{:S(2)}) copy-start(f32[4096]{0:T(1024)} %param.24) | copy-start | bytes 49156
  227.4 3.5 copy-start.5
  381.2 34.9 %copy-start.1 = (bf16[1024,1024]{1,0:T(8,128)(2,1)S(1)}, bf16[1024,1024]{1,0:T(8,128)(2,1)}, u32[]{:S(2)}) copy-start(bf16[1024,1024]{1,0:T(8,128)(2,1)} %param.22) | copy-start | bytes 6291460
where the time goes:
time: 417 us; the launch traced here: 416 us
  Pallas kernels  304 us (73%)
  matrix products  50.2 us (12%)
  local copies, waits for them, and re-layouts  27.5 us (7%)
  other arithmetic  24.4 us (6%)
  blocking collectives  5.52 us (1%)
  starting transfers between devices  4.47 us (1%)
    pallas_call x6, Pallas kernels, exchange(): pl.pallas_call(kernel, out_shape=jax.ShapeDtypeStruct(out_shape, x.dtype)...  234 us
    pallas_call x3, Pallas kernels, gather_ctx(): pl.pallas_call(kernel, out_shape=jax.ShapeDtypeStruct(out_shape, x.dtype)...  58.5 us
    dot_general x1, matrix products, on_device(): down = jnp.dot(activ, w_down[0], preferred_element_type=f32).astype(bf16)  28.8 us
    dot_general x1, matrix products, on_device(): gate_part = jnp.dot(segment, w_gate[0], preferred_element_type=f32)  13 us
  transfers between devices with their start and end apart: 2, of which 0 were waited for; matrix products, arithmetic and copies ran while one was open for 23% of the time, Pallas kernels for 73%

commit v1 on v0

v1 whole, which is shorter than its diff:
```python
import functools
import math

import jax
import jax.numpy as jnp
from jax import lax
from jax.experimental import pallas as pl
from jax.experimental.pallas import tpu as pltpu
from jax.sharding import PartitionSpec as P

epsilon = 1e-06
f32, bf16 = jnp.float32, jnp.bfloat16
MESH = pl.DeviceIdType.MESH
VMEM_LIMIT = 48 * 1024 * 1024
SMEM = pl.BlockSpec(memory_space=pltpu.SMEM)
LOCAL = pl.BlockSpec(memory_space=pltpu.VMEM)


def factors(count):
    inner = 2 ** (count.bit_length() // 2 - (1 if count.bit_length() % 2 == 0 else 0))
    return count // inner, inner


def ends_kernel(length, prompts, states, step_ref, signal_ref, rate_ref, into_ref, end_ref):
    tile = step_ref.shape[1:]
    for b in range(prompts):

        def chunk(i, carry):
            held, total = carry
            for u in range(4):
                row = (i * 4 + u) * prompts + b
                step = step_ref[row]
                inflow = step * signal_ref[row]
                held = tuple(
                    jnp.exp2(step * rate_ref[n]) * held[n] + inflow * into_ref[row * states + n]
                    for n in range(states)
                )
                total = total + step
            return held, total

        zero = jnp.zeros(tile, f32)
        held, total = lax.fori_loop(0, length // 4, chunk, ((zero,) * states, zero))
        for n in range(states):
            end_ref[b, n] = held[n]
        end_ref[b, states] = total


def scan_kernel(
    length, prompts, states, step_ref, signal_ref, rate_ref, into_ref, outof_ref, enter_ref, out_ref
):
    for b in range(prompts):

        def chunk(i, held):
            for u in range(4):
                row = (i * 4 + u) * prompts + b
                step = step_ref[row]
                inflow = step * signal_ref[row]
                held = tuple(
                    jnp.exp2(step * rate_ref[n]) * held[n] + inflow * into_ref[row * states + n]
                    for n in range(states)
                )
                terms = [held[n] * outof_ref[row * states + n] for n in range(states)]
                while len(terms) > 1:
                    terms = [p + q for p, q in zip(terms[::2], terms[1::2])]
                out_ref[row] = terms[0]
            return held

        lax.fori_loop(0, length // 4, chunk, tuple(enter_ref[b, n] for n in range(states)))


def wave(barrier, peers):
    for where in peers:
        pl.semaphore_signal(barrier, inc=1, device_id=where, device_id_type=MESH)
    pl.semaphore_wait(barrier, len(peers))


def push(src, dst, send_sem, recv_sem, where):
    copy = pltpu.make_async_remote_copy(
        src_ref=src,
        dst_ref=dst,
        send_sem=send_sem,
        recv_sem=recv_sem,
        device_id=where,
        device_id_type=MESH,
    )
    copy.start()
    return copy


def lanes_of(index, width):
    return pl.ds(pl.multiple_of(index * width, width), width)


def sending(kernel, out_shape, dtype, scratch, ident, *operands):
    return pl.pallas_call(
        kernel,
        out_shape=jax.ShapeDtypeStruct(out_shape, dtype),
        in_specs=[LOCAL] * len(operands),
        out_specs=LOCAL,
        scratch_shapes=scratch,
        compiler_params=pltpu.CompilerParams(
            collective_id=ident, has_side_effects=True, vmem_limit_bytes=VMEM_LIMIT
        ),
    )(*operands)


def gather_ctx(x, out_shape, count, target, ident):
    chips = count // 2

    def kernel(x_ref, o_ref, send_sem, recv_sem):
        me = lax.axis_index("ctx")
        chip, core = me // 2, lax.rem(me, 2)
        twin = {"ctx": chip * 2 + (1 - core)}
        others = [{"ctx": lax.rem(chip + k, chips) * 2 + core} for k in range(1, chips)]
        wave(pltpu.get_barrier_semaphore(), [twin] + others)
        across = [
            push(x_ref, target(o_ref, me), send_sem.at[k], recv_sem.at[k], others[k - 1])
            for k in range(1, chips)
        ]
        pending = [push(x_ref, target(o_ref, me), send_sem.at[0], recv_sem.at[0], twin)]
        target(o_ref, me)[...] = x_ref[...]
        for k in range(1, chips):
            across[k - 1].wait_recv()
            view = target(o_ref, lax.rem(chip + chips - k, chips) * 2 + core)
            slot = chips - 1 + k
            pending.append(push(view, view, send_sem.at[slot], recv_sem.at[slot], twin))
        for copy in across:
            copy.wait_send()
        for copy in pending:
            copy.wait()

    slots = pltpu.SemaphoreType.DMA((2 * chips - 1,))
    return sending(kernel, out_shape, x.dtype, [slots, slots], ident, x)


def scatter_sum(x, tokens, width, halves, count, parts, ident):
    outer, inner = factors(count)
    rows = tokens // parts

    def kernel(x_ref, o_ref, got1, part, got2, send1, recv1, send2, recv2):
        me = lax.axis_index("exp")
        o_me, i_me = me // inner, lax.rem(me, inner)
        near = [{"exp": o_me * inner + lax.rem(i_me + k, inner)} for k in range(1, inner)]
        far = [{"exp": lax.rem(o_me + j, outer) * inner + i_me} for j in range(1, outer)]
        wave(pltpu.get_barrier_semaphore(), near + far)

        def view(o, i, p):
            e = o * inner + i
            first = pl.multiple_of((e // halves) * tokens + p * rows, rows)
            return x_ref.at[pl.ds(first, rows), lanes_of(lax.rem(e, halves), width)]

        order = [(j % outer, p) for j in range(1, outer + 1) for p in range(parts)]
        first, sent = {}, []
        for j, p in order:
            for k in range(1, inner):
                copy = push(
                    view(lax.rem(o_me + j, outer), lax.rem(i_me + k, inner), p),
                    got1.at[k - 1, j, p],
                    send1.at[k - 1, j, p],
                    recv1.at[k - 1, j, p],
                    near[k - 1],
                )
                first[k, j, p] = copy
                sent.append(copy)

        def near_sum(j, p):
            total = view(lax.rem(o_me + j, outer), i_me, p)[...].astype(f32)
            for k in range(1, inner):
                first[k, j, p].wait_recv()
                total = total + got1[k - 1, j, p].astype(f32)
            return total

        second = {}
        for j, p in order:
            if j == 0:
                continue
            part[j - 1, p] = near_sum(j, p).astype(bf16)
            second[j, p] = push(
                part.at[j - 1, p],
                got2.at[j - 1, p],
                send2.at[j - 1, p],
                recv2.at[j - 1, p],
                far[j - 1],
            )
            sent.append(second[j, p])
        for p in range(parts):
            total = near_sum(0, p)
            for j in range(1, outer):
                second[j, p].wait_recv()
                total = total + got2[j - 1, p].astype(f32)
            o_ref[p * rows : (p + 1) * rows] = total
        for copy in sent:
            copy.wait_send()

    sem1 = pltpu.SemaphoreType.DMA((inner - 1, outer, parts))
    sem2 = pltpu.SemaphoreType.DMA((outer - 1, parts))
    scratch = [
        pltpu.VMEM((inner - 1, outer, parts, rows, width), bf16),
        pltpu.VMEM((outer - 1, parts, rows, width), bf16),
        pltpu.VMEM((outer - 1, parts, rows, width), bf16),
        sem1, sem1, sem2, sem2,
    ]
    return sending(kernel, (tokens, width), f32, scratch, ident, x)


def dispatch(x, n_ctx, n_exp, ident):
    _, cap, width = x.shape
    halves, chips = n_exp // n_ctx, n_ctx // 2

    def kernel(x_ref, o_ref, s_in, r_in, s_twin, r_twin, s_far, r_far, s_fwd, r_fwd):
        ctx, me = lax.axis_index("ctx"), lax.axis_index("exp")
        chip, core = ctx // 2, lax.rem(ctx, 2)
        twin = {"ctx": chip * 2 + (1 - core)}
        others = [{"ctx": lax.rem(chip + k, chips) * 2 + core} for k in range(1, chips)]
        peers = [{"exp": lax.rem(me + k, n_exp)} for k in range(1, n_exp)]
        wave(pltpu.get_barrier_semaphore(), [twin] + others + peers)

        def view(c, e):
            first = pl.multiple_of((e // halves) * cap, cap)
            return o_ref.at[pl.ds(first, cap), lanes_of(c * halves + lax.rem(e, halves), width)]

        arriving = [
            push(
                x_ref.at[lax.rem(me + k, n_exp)], view(ctx, me),
                s_in.at[k - 1], r_in.at[k - 1], peers[k - 1],
            )
            for k in range(1, n_exp)
        ]
        view(ctx, me)[...] = x_ref[me]
        far, near = {}, []
        for j in range(n_exp):
            if j:
                arriving[j - 1].wait_recv()
            mine = view(ctx, lax.rem(me + n_exp - j, n_exp))
            for k in range(1, chips):
                far[k, j] = push(
                    mine, mine, s_far.at[k - 1, j], r_far.at[k - 1, j], others[k - 1]
                )
            near.append(push(mine, mine, s_twin.at[j], r_twin.at[j], twin))
        for j in range(n_exp):
            for k in range(1, chips):
                far[k, j].wait_recv()
                owner = lax.rem(chip + chips - k, chips) * 2 + core
                theirs = view(owner, lax.rem(me + n_exp - j, n_exp))
                near.append(push(theirs, theirs, s_fwd.at[k - 1, j], r_fwd.at[k - 1, j], twin))
        for copy in arriving + list(far.values()):
            copy.wait_send()
        for copy in near:
            copy.wait()

    sem_in = pltpu.SemaphoreType.DMA((n_exp - 1,))
    sem_twin = pltpu.SemaphoreType.DMA((n_exp,))
    sem_far = pltpu.SemaphoreType.DMA((chips - 1, n_exp))
    scratch = [sem_in, sem_in, sem_twin, sem_twin, sem_far, sem_far, sem_far, sem_far]
    return sending(kernel, (n_ctx * cap, n_exp * width), x.dtype, scratch, ident, x)


def combine(x, weight, n_ctx, n_exp, ident):
    _, cap, features = x.shape
    width, chips = features // n_exp, n_ctx // 2

    def kernel(x_ref, w_ref, o_ref, got1, part, got2, ready, s1, r1, s2, r2, s3, r3):
        ctx, me = lax.axis_index("ctx"), lax.axis_index("exp")
        chip, core = ctx // 2, lax.rem(ctx, 2)
        twin = {"ctx": chip * 2 + (1 - core)}
        others = [{"ctx": lax.rem(chip + k, chips) * 2 + core} for k in range(1, chips)]
        peers = [{"exp": lax.rem(me + k, n_exp)} for k in range(1, n_exp)]
        wave(pltpu.get_barrier_semaphore(), [twin] + others + peers)
        columns = [lanes_of(lax.rem(me + j, n_exp), width) for j in range(n_exp)]
        turns = list(range(1, n_exp)) + [0]
        first, sent = {}, []
        for j in turns:
            for k in [*range(1, chips), 0]:
                block = lax.rem(chip + k, chips) * 2 + (1 - core)
                first[j, k] = push(
                    x_ref.at[block, :, columns[j]], got1.at[k, :, columns[j]],
                    s1.at[j, k], r1.at[j, k], twin,
                )
                sent.append(first[j, k])

        def near_sum(j, k):
            first[j, k].wait_recv()
            block = lax.rem(chip + k, chips) * 2 + core
            return x_ref[block, :, columns[j]].astype(f32) + got1[k, :, columns[j]].astype(f32)

        second = {}
        for j in turns:
            for k in range(1, chips):
                part[k - 1, :, columns[j]] = near_sum(j, k).astype(bf16)
                second[j, k] = push(
                    part.at[k - 1, :, columns[j]], got2.at[k - 1, :, columns[j]],
                    s2.at[j, k - 1], r2.at[j, k - 1], others[k - 1],
                )
                sent.append(second[j, k])
        last = []
        for j in turns:
            total = near_sum(j, 0)
            for k in range(1, chips):
                second[j, k].wait_recv()
                total = total + got2[k - 1, :, columns[j]].astype(f32)
            total = (total * w_ref[...]).astype(bf16)
            if j:
                ready[j - 1] = total
                last.append(
                    push(ready.at[j - 1], o_ref.at[me], s3.at[j - 1], r3.at[j - 1], peers[j - 1])
                )
            else:
                o_ref[me] = total
        for copy in sent:
            copy.wait_send()
        for copy in last:
            copy.wait()

    sem1 = pltpu.SemaphoreType.DMA((n_exp, chips))
    sem2 = pltpu.SemaphoreType.DMA((n_exp, chips - 1))
    sem3 = pltpu.SemaphoreType.DMA((n_exp - 1,))
    scratch = [
        pltpu.VMEM((chips, cap, features), bf16),
        pltpu.VMEM((chips - 1, cap, features), bf16),
        pltpu.VMEM((chips - 1, cap, features), bf16),
        pltpu.VMEM((n_exp - 1, cap, width), bf16),
        sem1, sem1, sem2, sem2, sem3, sem3,
    ]
    return sending(kernel, (n_exp, cap, width), bf16, scratch, ident, x, weight)


def block(ref, r):
    return ref.at[r]


def on_device(
    mixer_input,
    gate_in,
    step_size,
    decay_rate,
    state_in,
    state_out,
    skip,
    out_proj,
    hidden_in,
    norm_gain,
    w_gate,
    w_up,
    w_down,
    route_ids,
    route_weight,
):
    slab_len, prompts, channels = mixer_input.shape
    states = decay_rate.shape[0]
    tokens = slab_len * prompts
    n_ctx, n_exp = lax.axis_size("ctx"), lax.axis_size("exp")
    ctx, exp = lax.axis_index("ctx"), lax.axis_index("exp")
    share = hidden_in.shape[-1]
    halves = n_exp // n_ctx
    cap = 4 * tokens // (w_gate.shape[0] * n_exp)

    swap = [
        (c * n_exp + e, (e // halves) * n_exp + c * halves + e % halves)
        for c in range(n_ctx)
        for e in range(n_exp)
    ]
    hidden = lax.ppermute(hidden_in.reshape(tokens, share), ("ctx", "exp"), swap)
    routes = lax.all_gather(route_ids.reshape(tokens, -1), "ctx", axis=0)
    slab = exp // halves

    def selector(routed):
        named = jnp.any(routed[:, :, None] == jnp.arange(n_exp)[None, None, :], axis=1)
        place = jnp.cumsum(named.astype(jnp.int32), axis=0) - 1
        place = jnp.where(named, place, -1).T
        return place[:, None, :] == jnp.arange(cap)[None, :, None]

    lanes = (channels // 128, 128)
    signal = mixer_input.astype(f32).reshape(tokens, *lanes)
    step = step_size.reshape(tokens, *lanes)
    rate = (decay_rate * (-1.0 / math.log(2.0))).reshape(states, *lanes)
    into, outof = state_in.reshape(-1), state_out.reshape(-1)
    plain = pltpu.CompilerParams(vmem_limit_bytes=VMEM_LIMIT)
    ends = pl.pallas_call(
        functools.partial(ends_kernel, slab_len, prompts, states),
        out_shape=jax.ShapeDtypeStruct((prompts, states + 1) + lanes, f32),
        in_specs=[LOCAL, LOCAL, LOCAL, SMEM],
        out_specs=LOCAL,
        compiler_params=plain,
    )(step, signal, rate, into)
    ends = gather_ctx(ends, (n_ctx,) + ends.shape, n_ctx, block, 1)
    entering = jnp.zeros((prompts, states) + lanes, f32)
    for j in range(n_ctx - 1):
        longer = jnp.exp2(ends[j, :, states:] * rate[None]) * entering + ends[j, :, :states]
        entering = jnp.where(j < ctx, longer, entering)
    output = pl.pallas_call(
        functools.partial(scan_kernel, slab_len, prompts, states),
        out_shape=jax.ShapeDtypeStruct((tokens,) + lanes, f32),
        in_specs=[LOCAL, LOCAL, LOCAL, SMEM, SMEM, LOCAL],
        out_specs=LOCAL,
        compiler_params=plain,
    )(step, signal, rate, into, outof, entering)
    output = output.reshape(tokens, channels) + skip * mixer_input.astype(f32).reshape(tokens, -1)
    mixed = (output * jax.nn.silu(gate_in.astype(f32).reshape(tokens, -1))).astype(bf16)

    mixed = gather_ctx(
        mixed, (n_ctx * tokens, channels), n_ctx,
        lambda ref, c: ref.at[pl.ds(pl.multiple_of(c * tokens, tokens), tokens)], 2,
    )
    partial_value = jnp.dot(mixed, out_proj, preferred_element_type=f32).astype(bf16)
    projected = scatter_sum(partial_value, tokens, share, halves, n_exp, 2, 3)
    residual = hidden.astype(f32) + projected

    chosen = selector(lax.dynamic_index_in_dim(routes, slab, 0, keepdims=False))
    rows = jnp.dot(
        chosen.astype(bf16).reshape(n_exp * cap, tokens),
        residual.astype(bf16),
        preferred_element_type=f32,
    ).astype(bf16)
    rows = dispatch(rows.reshape(n_exp, cap, share), n_ctx, n_exp, 4)
    rows, residual = lax.optimization_barrier((rows, residual))
    residual_home = lax.ppermute(residual, ("ctx", "exp"), swap)
    rows = rows.astype(f32)
    scale = lax.rsqrt(jnp.mean(rows * rows, axis=1, keepdims=True) + epsilon)
    segment = (rows * scale * norm_gain).astype(bf16)

    gate_part = jnp.dot(segment, w_gate[0], preferred_element_type=f32)
    up_part = jnp.dot(segment, w_up[0], preferred_element_type=f32)
    activ = (jax.nn.silu(gate_part) * up_part).astype(bf16)
    down = jnp.dot(activ, w_down[0], preferred_element_type=f32).astype(bf16)

    own = selector(route_ids.reshape(tokens, -1))
    weights = route_weight.reshape(tokens, -1)
    strength = jnp.sum(jnp.where(route_ids.reshape(tokens, -1) == exp, weights, 0.0), axis=1)
    mine = lax.dynamic_index_in_dim(own, exp, 0, keepdims=False)
    slot_weight = jnp.sum(jnp.where(mine, strength[None, :], 0.0), axis=1)
    slot_weight = jnp.broadcast_to(slot_weight[:, None], (cap, share))
    back = combine(down.reshape(n_ctx, cap, -1), slot_weight, n_ctx, n_exp, 5)
    combined = lax.dot_general(
        own.astype(bf16).reshape(n_exp * cap, tokens),
        back.reshape(n_exp * cap, share),
        (((0,), (0,)), ((), ())),
        preferred_element_type=f32,
    )
    return (residual_home + combined).astype(bf16).reshape(slab_len, prompts, share)


def solution(mesh):
    placed = (
        P("ctx", None, "exp"),
        P("ctx", None, "exp"),
        P("ctx", None, "exp"),
        P(None, "exp"),
        P("ctx", None, None),
        P("ctx", None, None),
        P("exp"),
        P("exp", "ctx"),
        P("ctx", None, "exp"),
        P(),
        P("exp", None, "ctx"),
        P("exp", None, "ctx"),
        P("exp", "ctx", None),
        P("ctx", None, None),
        P("ctx", None, None),
    )
    return jax.shard_map(
        on_device, mesh=mesh, in_specs=placed, out_specs=P("ctx", None, "exp"), check_vma=False
    )
```

time: 417 us -> 227 us (0.54)
  Pallas kernels: 304 us -> 144 us
  other arithmetic: 24.4 us -> 7.22 us
  local copies, waits for them, and re-layouts: 27.5 us -> 19.7 us
  matrix products: 50.2 us -> 45.1 us
    pallas_call x9 -> x5, Pallas kernels: 293 us -> 133 us  [sending(): pl.pallas_call(kernel, out_shape=jax.ShapeDtypeStruct(out_shape, dtype),...]
    reduce_sum x4 -> x0, other arithmetic: 12.1 us -> none  [the longest x2 8.31 us: scatter_sum(): part = jnp.sum(got.astype(f32), axis=0).astype(bf16)]
    reshape x2 -> x0, local copies, waits for them, and re-layouts: 4.97 us -> none  [on_device(): partial_value.reshape(n_ctx, tokens, halves, share).transpose(0, 2, 1, 3)]
    another operation x4 -> x3, local copies, waits for them, and re-layouts: 4.83 us -> 0.22 us  [the longest x1 4.61 us: scatter_sum(): x = x.reshape(outer, inner, rows, columns).transpose(1, 0, 2, 3)]
  transfers between devices with their start and end apart: 2 -> 2, of which waited for: 0 -> 0; matrix products, arithmetic and copies ran while one was open for 23% -> 27% of each run, Pallas kernels for 73% -> 48%
where the time goes in v1:
time: 227 us
  Pallas kernels  144 us (63%)
  matrix products  45.1 us (20%)
  local copies, waits for them, and re-layouts  19.7 us (9%)
  other arithmetic  7.22 us (3%)
  blocking collectives  5.52 us (2%)
  starting transfers between devices  4.28 us (2%)
    pallas_call x5, Pallas kernels, sending(): pl.pallas_call(kernel, out_shape=jax.ShapeDtypeStruct(out_shape, dtype),...  133 us
    dot_general x1, matrix products, on_device(): down = jnp.dot(activ, w_down[0], preferred_element_type=f32).astype(bf16)  28.9 us
    dot_general x1, matrix products, on_device(): gate_part = jnp.dot(segment, w_gate[0], preferred_element_type=f32)  13 us
    unnamed x32, local copies, waits for them, and re-layouts  6.83 us
    pallas_call x1, Pallas kernels, on_device(): pl.pallas_call(functools.partial(scan_kernel, slab_len, prompts, states),...  6.36 us
    all_gather x1, blocking collectives, on_device(): routes = lax.all_gather(route_ids.reshape(tokens, -1), 'ctx', axis=0)  5.52 us
    pallas_call x1, Pallas kernels, on_device(): pl.pallas_call(functools.partial(ends_kernel, slab_len, prompts, states),...  4.59 us
  transfers between devices with their start and end apart: 2, of which 0 were waited for; matrix products, arithmetic and copies ran while one was open for 27% of the time, Pallas kernels for 48%

profile of v1, /device:TPU:11, one launch (start us, length us, event | category | flops | bytes accessed | tf_op | source)
XLA Modules:
  0.0 226.5 jit_solution(16507250272202157369)
XLA Ops:
  0.0 1.9 reshape.97
  1.9 3.6 %collective-permute-start = (bf16[256,512]{1,0:T(8,128)(2,1)}, bf16[256,512]{1,0:T(8,128)(2,1)}, u32[]{:S(2)}, u32[]{:S(2)}) collective-permute-start(bf16[256,512]{1,0:T(8,128)(2,1)} %reshape.97), channel_id=1, source_target_pairs={{0,0},{1,1},{2,8},{3,9},{4,16},{5,17},{6,24},{7,25},{8,2},{9,3},{1... | collective-permute-start | bytes 786440 | tf_op jit(solution)/shard_map/ppermute | solution.py:362
  5.5 1.3 reshape.99.signal_ref
  6.8 2.2 reshape.104
  10.1 5.5 %all_gather.3 = s32[4,256,2]{1,2,0:T(2,128)S(1)} all-gather(s32[1,256,2]{1,2,0:T(2,128)S(1)} %all_gather_reshape.3), channel_id=1, replica_groups=mesh['ctx'=4,'exp'=8] {'ctx'}, dimensions={0}, use_global_device_ids=true | all-gather | bytes 10240 | tf_op jit(solution)/shard_map/all_gather | solution.py:363
  16.6 3.1 %reshape.98.step_ref = f32[256,8,128]{2,1,0:T(8,128)} reshape(f32[128,2,1024]{2,1,0:T(2,128)} %param.17) | data formatting | bytes 2097152 | tf_op jit(solution)/shard_map/reshape | solution.py:374
  20.4 1.2 copy-done.3
  21.6 4.6 %shard_map.145.x_ref = f32[2,17,8,128]{3,2,1,0:T(8,128)S(1)} custom-call(f32[256,8,128]{2,1,0:T(8,128)S(1)} %copy-done.3, f32[256,8,128]{2,1,0:T(8,128)S(1)} %reshape.99.signal_ref, f32[16,8,128]{2,1,0:T(8,128)S(1)} %bitcast.88, f32[4096]{0:T(1024)S(1)} %reshape.101.into_ref), custom_call_target="tpu_custom_call" | custom-call | tf_op jit(solution)/shard_map/pallas_call | solution.py:378
  26.2 7.0 %shard_map.146 = f32[4,2,17,8,128]{4,3,2,1,0:T(8,128)S(1)} custom-call(f32[2,17,8,128]{3,2,1,0:T(8,128)S(1)} %shard_map.145.x_ref), custom_call_target="tpu_custom_call" | custom-call | tf_op jit(solution)/shard_map/pallas_call | solution.py:95
  34.0 2.2 reshape.114
  36.2 1.1 fusion.25.enter_ref
  37.3 1.2 copy-done.4
  38.6 6.4 %shard_map.147 = f32[256,8,128]{2,1,0:T(8,128)S(1)} custom-call(f32[256,8,128]{2,1,0:T(8,128)S(1)} %copy-done.4, f32[256,8,128]{2,1,0:T(8,128)S(1)} %reshape.99.signal_ref, f32[16,8,128]{2,1,0:T(8,128)S(1)} %bitcast.90, f32[4096]{0:T(1024)S(1)} %reshape.101.into_ref, f32[4096]{0:T(1024)S(1)} %reshape.102.outof_ref, f32[2,16,8,128]{3,2,1,0:T(8,128)S(1)} %fusion.25.enter_ref), custom_call_target="tpu_custom_call" | custom-call | tf_op jit(solution)/shard_map/pallas_call | solution.py:390
  44.9 2.0 fusion.23.x_ref
  47.0 15.8 %shard_map.148 = bf16[1024,1024]{1,0:T(8,128)(2,1)S(1)} custom-call(bf16[256,1024]{1,0:T(8,128)(2,1)S(1)} %fusion.23.x_ref), custom_call_target="tpu_custom_call" | custom-call | tf_op jit(solution)/shard_map/pallas_call | solution.py:95
  62.9 2.3 %convolution_convert_fusion.x_ref = bf16[1024,1024]{1,0:T(8,128)(2,1)S(1)} fusion(bf16[1024,1024]{1,0:T(8,128)(2,1)S(1)} %shard_map.148, bf16[1024,1024]{1,0:T(8,128)(2,1)S(1)} %copy-done), kind=kOutput, calls=%fused_computation.13 | convolution fusion | flops 2148532224 | bytes 6291456 | tf_op jit(solution)/shard_map/dot_general | solution.py:404
  65.2 31.9 %shard_map.149 = f32[256,512]{1,0:T(8,128)S(1)} custom-call(bf16[1024,1024]{1,0:T(8,128)(2,1)S(1)} %convolution_convert_fusion.x_ref), custom_call_target="tpu_custom_call" | custom-call | tf_op jit(solution)/shard_map/pallas_call | solution.py:95
  99.0 1.0 convert_add_fusion
  100.5 34.7 %shard_map.150 = bf16[512,4096]{1,0:T(8,128)(2,1)S(1)} custom-call(bf16[8,128,512]{2,1,0:T(8,128)(2,1)S(1)} %bitcast.85), custom_call_target="tpu_custom_call" | custom-call | tf_op jit(solution)/shard_map/pallas_call | solution.py:95
  135.9 0.9 fusion.6
  137.2 13.0 %fusion.4 = f32[512,1792]{1,0:T(8,128)} fusion(bf16[1,4096,1792]{2,1,0:T(8,128)(2,1)} %param.25, bf16[512,4096]{1,0:T(8,128)(2,1)S(1)} %shard_map.150, f32[4096]{0:T(1024)S(1)} %copy-done.13, f32[512]{0:T(512)S(1)} %add_rsqrt_fusion), kind=kOutput, calls=%fused_computation.4 | convolution fusion | flops 7524581376 | bytes 22562816 | tf_op jit(solution)/shard_map/dot_general | solution.py:421
  150.1 28.9 %fusion.9 = bf16[512,4096]{1,0:T(8,128)(2,1)} fusion(bf16[1,1792,4096]{2,1,0:T(8,128)(2,1)} %param.27, f32[512,1792]{1,0:T(8,128)} %fusion.4, bf16[1,4096,1792]{2,1,0:T(8,128)(2,1)} %param.26, bf16[512,4096]{1,0:T(8,128)(2,1)} %copy-done.2, f32[4096]{0:T(1024)S(1)} %copy-done.13, f32[512]{0:T(512)S(1)} %add_rsqrt_fusion), kind=kOutput, calls=%fused_computation.11 | convolution fusion | flops 15048376320 | bytes 41437184 | tf_op jit(solution)/shard_map/dot_general | solution.py:424
  179.1 2.2 copy-done.5
  181.3 43.9 %shard_map.151 = bf16[8,128,512]{2,1,0:T(8,128)(2,1)S(1)} custom-call(bf16[4,128,4096]{2,1,0:T(8,128)(2,1)S(1)} %bitcast.86, f32[128,512]{1,0:T(8,128)S(1)} %broadcast_in_dim.46.w_ref), custom_call_target="tpu_custom_call" | custom-call | tf_op jit(solution)/shard_map/pallas_call | solution.py:95
  (65 shorter events, 8.2 us)
Async XLA Ops:
  0.0 62.8 %copy-start = (bf16[1024,1024]{1,0:T(8,128)(2,1)S(1)}, bf16[1024,1024]{1,0:T(8,128)(2,1)}, u32[]{:S(2)}) copy-start(bf16[1024,1024]{1,0:T(8,128)(2,1)} %param.22) | copy-start | bytes 6291460
  0.0 19.7 %copy-start.7 = (f32[16,1024]{1,0:T(8,128)S(1)}, f32[16,1024]{1,0:T(8,128)}, u32[]{:S(2)}) copy-start(f32[16,1024]{1,0:T(8,128)} %param.18) | copy-start | bytes 196612
  0.0 19.7 %copy-start.8 = (f32[128,2,16]{0,2,1:T(8,128)S(1)}, f32[128,2,16]{0,2,1:T(8,128)}, u32[]{:S(2)}) copy-start(f32[128,2,16]{0,2,1:T(8,128)} %param.19) | copy-start | bytes 49156
  0.0 20.0 %copy-start.9 = (f32[128,2,16]{0,2,1:T(8,128)S(1)}, f32[128,2,16]{0,2,1:T(8,128)}, u32[]{:S(2)}) copy-start(f32[128,2,16]{0,2,1:T(8,128)} %param.20) | copy-start | bytes 49156
  1.9 97.1 %collective-permute-start = (bf16[256,512]{1,0:T(8,128)(2,1)}, bf16[256,512]{1,0:T(8,128)(2,1)}, u32[]{:S(2)}, u32[]{:S(2)}) collective-permute-start(bf16[256,512]{1,0:T(8,128)(2,1)} %reshape.97), channel_id=1, source_target_pairs={{0,0},{1,1},{2,8},{3,9},{4,16},{5,17},{6,24},{7,25},{8,2},{9,3},{1... | collective-permute-start | bytes 786440 | tf_op jit(solution)/shard_map/ppermute | solution.py:362
  20.4 1.2 copy-start.3
  21.6 23.3 %copy-start.11 = (f32[1024]{0:T(1024)S(1)}, f32[1024]{0:T(1024)}, u32[]{:S(2)}) copy-start(f32[1024]{0:T(1024)} %param.21) | copy-start | bytes 12292
  33.2 0.8 copy-start.6
  37.3 1.2 copy-start.4
  62.8 35.2 %copy-start.10 = (s32[128,2,2]{0,2,1:T(2,128)S(1)}, s32[128,2,2]{0,2,1:T(2,128)}, u32[]{:S(2)}) copy-start(s32[128,2,2]{0,2,1:T(2,128)} %param.28) | copy-start | bytes 6148
  62.9 35.2 %copy-start.12 = (f32[128,2,2]{0,2,1:T(2,128)S(1)}, f32[128,2,2]{0,2,1:T(2,128)}, u32[]{:S(2)}) copy-start(f32[128,2,2]{0,2,1:T(2,128)} %param.29) | copy-start | bytes 6148
  100.5 36.6 %copy-start.13 = (f32[4096]{0:T(1024)S(1)}, f32[4096]{0:T(1024)}, u32[]{:S(2)}) copy-start(f32[4096]{0:T(1024)} %param.24) | copy-start | bytes 49156
  135.2 1.9 copy-start.2
  135.2 90.0 %collective-permute-start.1 = (f32[256,512]{1,0:T(8,128)S(1)}, f32[256,512]{1,0:T(8,128)S(1)}, u32[]{:S(2)}, u32[]{:S(2)}) collective-permute-start(f32[256,512]{1,0:T(8,128)S(1)} %convert_add_fusion), channel_id=1, source_target_pairs={{0,0},{1,1},{2,8},{3,9},{4,16},{5,17},{6,24},{7,25},{8,2},{9,3},{1... | collective-permute-start | bytes 1572872 | tf_op jit(solution)/shard_map/ppermute | solution.py:416
  150.1 76.4 %copy-start.1 = (bf16[1024,1024]{1,0:T(8,128)(2,1)S(1)}, bf16[1024,1024]{1,0:T(8,128)(2,1)}, u32[]{:S(2)}) copy-start(bf16[1024,1024]{1,0:T(8,128)(2,1)} %param.22) | copy-start | bytes 6291460
  179.1 2.2 copy-start.5

commit v2 on v1

--- a/solution.py
+++ b/solution.py
@@ -21,7 +21,9 @@
     return count // inner, inner
 
 
-def ends_kernel(length, prompts, states, step_ref, signal_ref, rate_ref, into_ref, end_ref):
+def ends_kernel(
+    length, prompts, states, step_ref, signal_ref, rate_ref, into_ref, route_ref, end_ref
+):
     tile = step_ref.shape[1:]
     for b in range(prompts):
 
@@ -41,8 +43,9 @@
         zero = jnp.zeros(tile, f32)
         held, total = lax.fori_loop(0, length // 4, chunk, ((zero,) * states, zero))
         for n in range(states):
-            end_ref[b, n] = held[n]
-        end_ref[b, states] = total
+            end_ref[b * (states + 1) + n] = held[n]
+        end_ref[b * (states + 1) + states] = total
+    end_ref[prompts * (states + 1) :] = route_ref[...]
 
 
 def scan_kernel(
@@ -66,6 +69,68 @@
             return held
 
         lax.fori_loop(0, length // 4, chunk, tuple(enter_ref[b, n] for n in range(states)))
+
+
+def act_kernel(rows_ref, gain_ref, gate_ref, up_ref, out_ref, normed):
+    count, features = rows_ref.shape
+
+    @pl.when(pl.program_id(0) == 0)
+    def _():
+        def norm(i, _):
+            here = pl.ds(pl.multiple_of(i * 32, 32), 32)
+            rows = rows_ref[here].astype(f32)
+            scale = lax.rsqrt(jnp.sum(rows * rows, axis=1, keepdims=True) / features + epsilon)
+            normed[here] = (rows * scale * gain_ref[...]).astype(bf16)
+            return 0
+
+        lax.fori_loop(0, count // 32, norm, 0)
+
+    gate_part = jnp.dot(normed[...], gate_ref[0], preferred_element_type=f32)
+    up_part = jnp.dot(normed[...], up_ref[0], preferred_element_type=f32)
+    out_ref[...] = (gate_part / (1.0 + jnp.exp(-gate_part)) * up_part).astype(bf16)
+
+
+def expert_act(rows, gain, w_gate, w_up):
+    count, features = rows.shape
+    hidden = w_gate.shape[2]
+    tile = 256 if hidden % 256 == 0 else 128
+    weights = pl.BlockSpec((1, features, tile), lambda i: (0, 0, i))
+    return pl.pallas_call(
+        act_kernel,
+        grid=(hidden // tile,),
+        out_shape=jax.ShapeDtypeStruct((count, hidden), bf16),
+        in_specs=[
+            pl.BlockSpec((count, features), lambda i: (0, 0)),
+            pl.BlockSpec((1, features), lambda i: (0, 0)),
+            weights,
+            weights,
+        ],
+        out_specs=pl.BlockSpec((count, tile), lambda i: (0, i)),
+        scratch_shapes=[pltpu.VMEM((count, features), bf16)],
+        compiler_params=pltpu.CompilerParams(vmem_limit_bytes=VMEM_LIMIT),
+    )(rows, gain, w_gate, w_up)
+
+
+def down_kernel(act_ref, weight_ref, out_ref):
+    out_ref[...] = jnp.dot(
+        act_ref[...], weight_ref[0], preferred_element_type=f32
+    ).astype(bf16)
+
+
+def expert_down(activ, w_down):
+    count, hidden = activ.shape
+    features = w_down.shape[2]
+    return pl.pallas_call(
+        down_kernel,
+        grid=(features // 512,),
+        out_shape=jax.ShapeDtypeStruct((count, features), bf16),
+        in_specs=[
+            pl.BlockSpec((count, hidden), lambda i: (0, 0)),
+            pl.BlockSpec((1, hidden, 512), lambda i: (0, 0, i)),
+        ],
+        out_specs=pl.BlockSpec((count, 512), lambda i: (0, i)),
+        compiler_params=pltpu.CompilerParams(vmem_limit_bytes=VMEM_LIMIT),
+    )(activ, w_down)
 
 
 def wave(barrier, peers):
@@ -360,7 +425,6 @@
         for e in range(n_exp)
     ]
     hidden = lax.ppermute(hidden_in.reshape(tokens, share), ("ctx", "exp"), swap)
-    routes = lax.all_gather(route_ids.reshape(tokens, -1), "ctx", axis=0)
     slab = exp // halves
 
     def selector(routed):
@@ -375,14 +439,20 @@
     rate = (decay_rate * (-1.0 / math.log(2.0))).reshape(states, *lanes)
     into, outof = state_in.reshape(-1), state_out.reshape(-1)
     plain = pltpu.CompilerParams(vmem_limit_bytes=VMEM_LIMIT)
+    named = route_ids.reshape(-1).astype(f32)
+    named = jnp.pad(named, (0, -named.size % channels)).reshape(-1, *lanes)
+    summary = prompts * (states + 1)
     ends = pl.pallas_call(
         functools.partial(ends_kernel, slab_len, prompts, states),
-        out_shape=jax.ShapeDtypeStruct((prompts, states + 1) + lanes, f32),
-        in_specs=[LOCAL, LOCAL, LOCAL, SMEM],
+        out_shape=jax.ShapeDtypeStruct((summary + named.shape[0],) + lanes, f32),
+        in_specs=[LOCAL, LOCAL, LOCAL, SMEM, LOCAL],
         out_specs=LOCAL,
         compiler_params=plain,
-    )(step, signal, rate, into)
+    )(step, signal, rate, into, named)
     ends = gather_ctx(ends, (n_ctx,) + ends.shape, n_ctx, block, 1)
+    routes = ends[:, summary:].reshape(n_ctx, -1)[:, : route_ids.size].astype(jnp.int32)
+    routes = routes.reshape(n_ctx, tokens, -1)
+    ends = ends[:, :summary].reshape((n_ctx, prompts, states + 1) + lanes)
     entering = jnp.zeros((prompts, states) + lanes, f32)
     for j in range(n_ctx - 1):
         longer = jnp.exp2(ends[j, :, states:] * rate[None]) * entering + ends[j, :, :states]
@@ -414,14 +484,8 @@
     rows = dispatch(rows.reshape(n_exp, cap, share), n_ctx, n_exp, 4)
     rows, residual = lax.optimization_barrier((rows, residual))
     residual_home = lax.ppermute(residual, ("ctx", "exp"), swap)
-    rows = rows.astype(f32)
-    scale = lax.rsqrt(jnp.mean(rows * rows, axis=1, keepdims=True) + epsilon)
-    segment = (rows * scale * norm_gain).astype(bf16)
-
-    gate_part = jnp.dot(segment, w_gate[0], preferred_element_type=f32)
-    up_part = jnp.dot(segment, w_up[0], preferred_element_type=f32)
-    activ = (jax.nn.silu(gate_part) * up_part).astype(bf16)
-    down = jnp.dot(activ, w_down[0], preferred_element_type=f32).astype(bf16)
+    activ = expert_act(rows, norm_gain[None, :], w_gate, w_up)
+    down = expert_down(activ, w_down)
 
     own = selector(route_ids.reshape(tokens, -1))
     weights = route_weight.reshape(tokens, -1)

time: 227 us -> 221 us (0.974)
  matrix products: 45.1 us -> 6.15 us
  Pallas kernels: 144 us -> 179 us
  blocking collectives: 5.52 us -> 0 us
  local copies, waits for them, and re-layouts: 19.7 us -> 24.3 us
    dot_general x2 -> x0, matrix products: 41.9 us -> none  [the longest x1 28.9 us: on_device(): down = jnp.dot(activ, w_down[0], preferred_element_type=f32).astype(bf16)]
    pallas_call x0 -> x2, Pallas kernels: none -> 33.6 us  [the longest x1 21.6 us: expert_act(): pl.pallas_call(act_kernel, grid=(hidden // tile,), out_shape=jax.ShapeDty...]
    all_gather x1 -> x0, blocking collectives: 5.52 us -> none  [on_device(): routes = lax.all_gather(route_ids.reshape(tokens, -1), 'ctx', axis=0)]
    dot_general x1, matrix products: 2.33 us -> 5.22 us  [on_device(): jnp.dot(mixed, out_proj, preferred_element_type=f32).astype(bf16)]
    unnamed x32 -> x36, local copies, waits for them, and re-layouts: 6.83 us -> 6.47 us
  transfers between devices with their start and end apart: 2 -> 2, of which waited for: 0 -> 0; matrix products, arithmetic and copies ran while one was open for 27% -> 12% of each run, Pallas kernels for 48% -> 65%
where the time goes in v2:
time: 221 us; the launch traced here: 220 us
  Pallas kernels  179 us (81%)
  local copies, waits for them, and re-layouts  24.3 us (11%)
  matrix products  6.15 us (3%)
  other arithmetic  5.78 us (3%)
  starting transfers between devices  4.6 us (2%)
    pallas_call x5, Pallas kernels, sending(): pl.pallas_call(kernel, out_shape=jax.ShapeDtypeStruct(out_shape, dtype),...  135 us
    pallas_call x1, Pallas kernels, expert_act(): pl.pallas_call(act_kernel, grid=(hidden // tile,), out_shape=jax.ShapeDty...  21.6 us
    pallas_call x1, Pallas kernels, expert_down(): pl.pallas_call(down_kernel, grid=(features // 512,), out_shape=jax.ShapeD...  11.9 us
    unnamed x36, local copies, waits for them, and re-layouts  6.47 us
    pallas_call x1, Pallas kernels, on_device(): pl.pallas_call(functools.partial(scan_kernel, slab_len, prompts, states),...  6.36 us
    dot_general x1, matrix products, on_device(): jnp.dot(mixed, out_proj, preferred_element_type=f32).astype(bf16)  5.22 us
    pallas_call x1, Pallas kernels, on_device(): pl.pallas_call(functools.partial(ends_kernel, slab_len, prompts, states),...  4.58 us
  transfers between devices with their start and end apart: 2, of which 0 were waited for; matrix products, arithmetic and copies ran while one was open for 12% of the time, Pallas kernels for 65%

profile of v2, /device:TPU:11, one launch (start us, length us, event | category | flops | bytes accessed | tf_op | source)
XLA Modules:
  0.0 220.4 jit_solution(13409678873014160758)
XLA Ops:
  0.0 1.9 reshape.109
  1.9 3.7 %collective-permute-start = (bf16[256,512]{1,0:T(8,128)(2,1)}, bf16[256,512]{1,0:T(8,128)(2,1)}, u32[]{:S(2)}, u32[]{:S(2)}) collective-permute-start(bf16[256,512]{1,0:T(8,128)(2,1)} %reshape.109), channel_id=1, source_target_pairs={{0,0},{1,1},{2,8},{3,9},{4,16},{5,17},{6,24},{7,25},{8,2},{9,3},{1... | collective-permute-start | bytes 786440 | tf_op jit(solution)/shard_map/ppermute | solution.py:427
  5.6 2.1 reshape.100.step_ref
  7.7 2.3 %reshape.101.signal_ref = f32[256,8,128]{2,1,0:T(8,128)} reshape(bf16[128,2,1024]{2,1,0:T(2,128)(2,1)} %param.15) | data formatting | bytes 1572864 | tf_op jit(solution)/shard_map/reshape | solution.py:437
  10.8 1.2 copy-done.2
  12.0 4.6 %shard_map.145.x_ref = f32[35,8,128]{2,1,0:T(8,128)S(1)} custom-call(f32[256,8,128]{2,1,0:T(8,128)S(1)} %reshape.100.step_ref, f32[256,8,128]{2,1,0:T(8,128)S(1)} %copy-done.2, f32[16,8,128]{2,1,0:T(8,128)S(1)} %bitcast.82, f32[4096]{0:T(1024)S(1)} %reshape.103.into_ref, f32[1,8,128]{2,1,0:T(8,128)S(1)} %pad_bitcast_fusion.route_ref), custom_call_target="tpu_custom_call" | custom-call | tf_op jit(solution)/shard_map/pallas_call | solution.py:445
  16.6 7.5 %shard_map.146 = f32[4,35,8,128]{3,2,1,0:T(8,128)S(1)} custom-call(f32[35,8,128]{2,1,0:T(8,128)S(1)} %shard_map.145.x_ref), custom_call_target="tpu_custom_call" | custom-call | tf_op jit(solution)/shard_map/pallas_call | solution.py:160
  24.9 2.2 %reshape.113 = f32[256,1024]{1,0:T(8,128)} reshape(bf16[128,2,1024]{2,1,0:T(2,128)(2,1)} %param.15) | data formatting | bytes 1572864 | tf_op jit(solution)/shard_map/reshape | solution.py:467
  27.9 1.0 copy.46
  30.0 1.0 constant_dynamic-slice_fusion
  31.0 1.1 copy.42
  33.9 2.2 reshape.123
  36.1 1.1 fusion.6.enter_ref
  37.2 1.2 copy-done.3
  38.5 6.4 %shard_map.147 = f32[256,8,128]{2,1,0:T(8,128)S(1)} custom-call(f32[256,8,128]{2,1,0:T(8,128)S(1)} %reshape.100.step_ref, f32[256,8,128]{2,1,0:T(8,128)S(1)} %copy-done.3, f32[16,8,128]{2,1,0:T(8,128)S(1)} %bitcast.84, f32[4096]{0:T(1024)S(1)} %reshape.103.into_ref, f32[4096]{0:T(1024)S(1)} %reshape.110.outof_ref, f32[2,16,8,128]{3,2,1,0:T(8,128)S(1)} %fusion.6.enter_ref), custom_call_target="tpu_custom_call" | custom-call | tf_op jit(solution)/shard_map/pallas_call | solution.py:460
  45.4 15.8 %shard_map.148 = bf16[1024,1024]{1,0:T(8,128)(2,1)S(1)} custom-call(bf16[256,1024]{1,0:T(8,128)(2,1)S(1)} %fusion.3.x_ref), custom_call_target="tpu_custom_call" | custom-call | tf_op jit(solution)/shard_map/pallas_call | solution.py:160
  61.3 1.3 copy-done.4
  63.6 5.2 %convolution_convert_fusion.x_ref = bf16[1024,1024]{1,0:T(8,128)(2,1)} fusion(bf16[1024,1024]{1,0:T(8,128)(2,1)} %copy-done.4, bf16[1024,1024]{1,0:T(8,128)(2,1)S(1)} %copy-done), kind=kOutput, calls=%fused_computation | convolution fusion | flops 2148532224 | bytes 6291456 | tf_op jit(solution)/shard_map/dot_general | solution.py:474
  68.9 1.6 copy-done.5
  70.5 31.8 %shard_map.149 = f32[256,512]{1,0:T(8,128)S(1)} custom-call(bf16[1024,1024]{1,0:T(8,128)(2,1)S(1)} %copy-done.5), custom_call_target="tpu_custom_call" | custom-call | tf_op jit(solution)/shard_map/pallas_call | solution.py:160
  104.4 35.1 %shard_map.150.rows_ref = bf16[512,4096]{1,0:T(8,128)(2,1)S(1)} custom-call(bf16[8,128,512]{2,1,0:T(8,128)(2,1)S(1)} %bitcast.80), custom_call_target="tpu_custom_call" | custom-call | tf_op jit(solution)/shard_map/pallas_call | solution.py:160
  141.0 21.6 %shard_map.151.act_ref = bf16[512,1792]{1,0:T(8,128)(2,1)S(1)} custom-call(bf16[512,4096]{1,0:T(8,128)(2,1)S(1)} %shard_map.150.rows_ref, f32[1,4096]{1,0:T(1,128)S(1)} %bitcast.85, bf16[1,4096,1792]{2,1,0:T(8,128)(2,1)} %gate_ref.1, bf16[1,4096,1792]{2,1,0:T(8,128)(2,1)} %up_ref.1), custom_call_target="tpu_custom_call" | custom-call | tf_op jit(solution)/shard_map/pallas_call | solution.py:98
  162.6 11.9 %shard_map.152 = bf16[512,4096]{1,0:T(8,128)(2,1)S(1)} custom-call(bf16[512,1792]{1,0:T(8,128)(2,1)S(1)} %shard_map.151.act_ref, bf16[1,1792,4096]{2,1,0:T(8,128)(2,1)} %weight_ref.1), custom_call_target="tpu_custom_call" | custom-call | tf_op jit(solution)/shard_map/pallas_call | solution.py:123
  174.7 44.4 %shard_map.153 = bf16[8,128,512]{2,1,0:T(8,128)(2,1)S(1)} custom-call(bf16[4,128,4096]{2,1,0:T(8,128)(2,1)S(1)} %bitcast.79, f32[128,512]{1,0:T(8,128)S(1)} %broadcast_in_dim.48.w_ref), custom_call_target="tpu_custom_call" | custom-call | tf_op jit(solution)/shard_map/pallas_call | solution.py:160
  (74 shorter events, 11.6 us)
Async XLA Ops:
  0.0 63.6 %copy-start = (bf16[1024,1024]{1,0:T(8,128)(2,1)S(1)}, bf16[1024,1024]{1,0:T(8,128)(2,1)}, u32[]{:S(2)}) copy-start(bf16[1024,1024]{1,0:T(8,128)(2,1)} %param.22) | copy-start | bytes 6291460
  0.0 10.0 %copy-start.10 = (f32[16,1024]{1,0:T(8,128)S(1)}, f32[16,1024]{1,0:T(8,128)}, u32[]{:S(2)}) copy-start(f32[16,1024]{1,0:T(8,128)} %param.18) | copy-start | bytes 196612
  1.9 8.2 %copy-start.12 = (f32[128,2,16]{0,2,1:T(8,128)S(1)}, f32[128,2,16]{0,2,1:T(8,128)}, u32[]{:S(2)}) copy-start(f32[128,2,16]{0,2,1:T(8,128)} %param.19) | copy-start | bytes 49156
  1.9 101.0 %collective-permute-start = (bf16[256,512]{1,0:T(8,128)(2,1)}, bf16[256,512]{1,0:T(8,128)(2,1)}, u32[]{:S(2)}, u32[]{:S(2)}) collective-permute-start(bf16[256,512]{1,0:T(8,128)(2,1)} %reshape.109), channel_id=1, source_target_pairs={{0,0},{1,1},{2,8},{3,9},{4,16},{5,17},{6,24},{7,25},{8,2},{9,3},{1... | collective-permute-start | bytes 786440 | tf_op jit(solution)/shard_map/ppermute | solution.py:427
  5.6 4.7 %copy-start.11 = (s32[128,2,2]{0,2,1:T(2,128)S(1)}, s32[128,2,2]{0,2,1:T(2,128)}, u32[]{:S(2)}) copy-start(s32[128,2,2]{0,2,1:T(2,128)} %param.28) | copy-start | bytes 6148
  10.8 1.2 copy-start.2
  24.9 8.0 %copy-start.13 = (f32[128,2,16]{0,2,1:T(8,128)S(1)}, f32[128,2,16]{0,2,1:T(8,128)}, u32[]{:S(2)}) copy-start(f32[128,2,16]{0,2,1:T(8,128)} %param.20) | copy-start | bytes 49156
  36.1 8.7 %copy-start.14 = (f32[1024]{0:T(1024)S(1)}, f32[1024]{0:T(1024)}, u32[]{:S(2)}) copy-start(f32[1024]{0:T(1024)} %param.21) | copy-start | bytes 12292
  37.2 1.2 copy-start.3
  38.5 6.4 %copy-start.7 = (f32[256,1024]{1,0:T(8,128)S(1)}, f32[256,1024]{1,0:T(8,128)}, u32[]{:S(2)}) copy-start(f32[256,1024]{1,0:T(8,128)} %reshape.113) | copy-start | bytes 3145732
  38.5 6.4 %copy-start.8 = (f32[256,1024]{1,0:T(8,128)S(1)}, f32[256,1024]{1,0:T(8,128)}, u32[]{:S(2)}) copy-start(f32[256,1024]{1,0:T(8,128)} %reshape.123) | copy-start | bytes 3145732
  45.4 17.2 %copy-start.9 = (s32[128,2,2]{1,0,2:T(8,128)S(1)}, s32[128,2,2]{1,0,2:T(8,128)}, u32[]{:S(2)}) copy-start(s32[128,2,2]{1,0,2:T(8,128)} %copy.44) | copy-start | bytes 6148
  45.4 18.2 %copy-start.15 = (f32[128,2,2]{0,2,1:T(2,128)S(1)}, f32[128,2,2]{0,2,1:T(2,128)}, u32[]{:S(2)}) copy-start(f32[128,2,2]{0,2,1:T(2,128)} %param.29) | copy-start | bytes 6148
  61.3 1.4 copy-start.4
  68.9 1.6 copy-start.5
  104.4 36.6 %copy-start.6 = (f32[4096]{0:T(1024)S(1)}, f32[4096]{0:T(1024)}, u32[]{:S(2)}) copy-start(f32[4096]{0:T(1024)} %param.24) | copy-start | bytes 49156
  139.6 79.5 %collective-permute-start.1 = (f32[256,512]{1,0:T(8,128)S(1)}, f32[256,512]{1,0:T(8,128)S(1)}, u32[]{:S(2)}, u32[]{:S(2)}) collective-permute-start(f32[256,512]{1,0:T(8,128)S(1)} %convert_add_fusion), channel_id=1, source_target_pairs={{0,0},{1,1},{2,8},{3,9},{4,16},{5,17},{6,24},{7,25},{8,2},{9,3},{1... | collective-permute-start | bytes 1572872 | tf_op jit(solution)/shard_map/ppermute | solution.py:486
  174.7 45.7 %copy-start.1 = (bf16[1024,1024]{1,0:T(8,128)(2,1)S(1)}, bf16[1024,1024]{1,0:T(8,128)(2,1)}, u32[]{:S(2)}) copy-start(bf16[1024,1024]{1,0:T(8,128)(2,1)} %param.22) | copy-start | bytes 6291460

commit v3 on v2

--- a/solution.py
+++ b/solution.py
@@ -150,6 +150,10 @@
     )
     copy.start()
     return copy
+
+
+def far_first(count):
+    return sorted(range(1, count), key=lambda k: -min(k, count - k))
 
 
 def lanes_of(index, width):
@@ -284,31 +288,32 @@
             first = pl.multiple_of((e // halves) * cap, cap)
             return o_ref.at[pl.ds(first, cap), lanes_of(c * halves + lax.rem(e, halves), width)]
 
-        arriving = [
-            push(
+        arriving = {
+            k: push(
                 x_ref.at[lax.rem(me + k, n_exp)], view(ctx, me),
                 s_in.at[k - 1], r_in.at[k - 1], peers[k - 1],
             )
-            for k in range(1, n_exp)
-        ]
+            for k in far_first(n_exp)
+        }
         view(ctx, me)[...] = x_ref[me]
+        turns = [0] + far_first(n_exp)[::-1]
         far, near = {}, []
-        for j in range(n_exp):
+        for j in turns:
             if j:
-                arriving[j - 1].wait_recv()
+                arriving[j].wait_recv()
             mine = view(ctx, lax.rem(me + n_exp - j, n_exp))
             for k in range(1, chips):
                 far[k, j] = push(
                     mine, mine, s_far.at[k - 1, j], r_far.at[k - 1, j], others[k - 1]
                 )
             near.append(push(mine, mine, s_twin.at[j], r_twin.at[j], twin))
-        for j in range(n_exp):
+        for j in turns:
             for k in range(1, chips):
                 far[k, j].wait_recv()
                 owner = lax.rem(chip + chips - k, chips) * 2 + core
                 theirs = view(owner, lax.rem(me + n_exp - j, n_exp))
                 near.append(push(theirs, theirs, s_fwd.at[k - 1, j], r_fwd.at[k - 1, j], twin))
-        for copy in arriving + list(far.values()):
+        for copy in [*arriving.values(), *far.values()]:
             copy.wait_send()
         for copy in near:
             copy.wait()
@@ -332,7 +337,7 @@
         peers = [{"exp": lax.rem(me + k, n_exp)} for k in range(1, n_exp)]
         wave(pltpu.get_barrier_semaphore(), [twin] + others + peers)
         columns = [lanes_of(lax.rem(me + j, n_exp), width) for j in range(n_exp)]
-        turns = list(range(1, n_exp)) + [0]
+        turns = far_first(n_exp) + [0]
         first, sent = {}, []
         for j in turns:
             for k in [*range(1, chips), 0]:
@@ -472,7 +477,7 @@
         lambda ref, c: ref.at[pl.ds(pl.multiple_of(c * tokens, tokens), tokens)], 2,
     )
     partial_value = jnp.dot(mixed, out_proj, preferred_element_type=f32).astype(bf16)
-    projected = scatter_sum(partial_value, tokens, share, halves, n_exp, 2, 3)
+    projected = scatter_sum(partial_value, tokens, share, halves, n_exp, 4, 3)
     residual = hidden.astype(f32) + projected
 
     chosen = selector(lax.dynamic_index_in_dim(routes, slab, 0, keepdims=False))

time: 221 us -> 224 us (1.014)
  transfers between devices with their start and end apart: 2 -> 2, of which waited for: 0 -> 0; matrix products, arithmetic and copies ran while one was open for 12% -> 12% of each run, Pallas kernels for 65% -> 59%
where the time goes in v3:
time: 224 us; the launch traced here: 222 us
  Pallas kernels  180 us (80%)
  local copies, waits for them, and re-layouts  24.3 us (11%)
  matrix products  6.15 us (3%)
  other arithmetic  5.78 us (3%)
  starting transfers between devices  4.6 us (2%)
    pallas_call x5, Pallas kernels, sending(): pl.pallas_call(kernel, out_shape=jax.ShapeDtypeStruct(out_shape, dtype),...  136 us
    pallas_call x1, Pallas kernels, expert_act(): pl.pallas_call(act_kernel, grid=(hidden // tile,), out_shape=jax.ShapeDty...  21.6 us
    pallas_call x1, Pallas kernels, expert_down(): pl.pallas_call(down_kernel, grid=(features // 512,), out_shape=jax.ShapeD...  11.9 us
    unnamed x36, local copies, waits for them, and re-layouts  6.47 us
    pallas_call x1, Pallas kernels, on_device(): pl.pallas_call(functools.partial(scan_kernel, slab_len, prompts, states),...  6.36 us
    dot_general x1, matrix products, on_device(): jnp.dot(mixed, out_proj, preferred_element_type=f32).astype(bf16)  5.22 us
    pallas_call x1, Pallas kernels, on_device(): pl.pallas_call(functools.partial(ends_kernel, slab_len, prompts, states),...  4.58 us
  transfers between devices with their start and end apart: 2, of which 0 were waited for; matrix products, arithmetic and copies ran while one was open for 12% of the time, Pallas kernels for 59%

profile of v3, /device:TPU:11, one launch (start us, length us, event | category | flops | bytes accessed | tf_op | source)
XLA Modules:
  0.0 221.6 jit_solution(11483275738382331734)
XLA Ops:
  0.0 1.9 reshape.109
  1.9 3.7 %collective-permute-start = (bf16[256,512]{1,0:T(8,128)(2,1)}, bf16[256,512]{1,0:T(8,128)(2,1)}, u32[]{:S(2)}, u32[]{:S(2)}) collective-permute-start(bf16[256,512]{1,0:T(8,128)(2,1)} %reshape.109), channel_id=1, source_target_pairs={{0,0},{1,1},{2,8},{3,9},{4,16},{5,17},{6,24},{7,25},{8,2},{9,3},{1... | collective-permute-start | bytes 786440 | tf_op jit(solution)/shard_map/ppermute | solution.py:432
  5.6 2.1 reshape.100.step_ref
  7.7 2.3 %reshape.101.signal_ref = f32[256,8,128]{2,1,0:T(8,128)} reshape(bf16[128,2,1024]{2,1,0:T(2,128)(2,1)} %param.15) | data formatting | bytes 1572864 | tf_op jit(solution)/shard_map/reshape | solution.py:442
  10.8 1.2 copy-done.2
  12.0 4.6 %shard_map.145.x_ref = f32[35,8,128]{2,1,0:T(8,128)S(1)} custom-call(f32[256,8,128]{2,1,0:T(8,128)S(1)} %reshape.100.step_ref, f32[256,8,128]{2,1,0:T(8,128)S(1)} %copy-done.2, f32[16,8,128]{2,1,0:T(8,128)S(1)} %bitcast.82, f32[4096]{0:T(1024)S(1)} %reshape.103.into_ref, f32[1,8,128]{2,1,0:T(8,128)S(1)} %pad_bitcast_fusion.route_ref), custom_call_target="tpu_custom_call" | custom-call | tf_op jit(solution)/shard_map/pallas_call | solution.py:450
  16.6 7.5 %shard_map.146 = f32[4,35,8,128]{3,2,1,0:T(8,128)S(1)} custom-call(f32[35,8,128]{2,1,0:T(8,128)S(1)} %shard_map.145.x_ref), custom_call_target="tpu_custom_call" | custom-call | tf_op jit(solution)/shard_map/pallas_call | solution.py:164
  24.9 2.2 %reshape.113 = f32[256,1024]{1,0:T(8,128)} reshape(bf16[128,2,1024]{2,1,0:T(2,128)(2,1)} %param.15) | data formatting | bytes 1572864 | tf_op jit(solution)/shard_map/reshape | solution.py:472
  27.9 1.0 copy.46
  30.0 1.0 constant_dynamic-slice_fusion
  31.0 1.1 copy.42
  33.9 2.2 reshape.123
  36.1 1.1 fusion.6.enter_ref
  37.2 1.2 copy-done.3
  38.5 6.4 %shard_map.147 = f32[256,8,128]{2,1,0:T(8,128)S(1)} custom-call(f32[256,8,128]{2,1,0:T(8,128)S(1)} %reshape.100.step_ref, f32[256,8,128]{2,1,0:T(8,128)S(1)} %copy-done.3, f32[16,8,128]{2,1,0:T(8,128)S(1)} %bitcast.84, f32[4096]{0:T(1024)S(1)} %reshape.103.into_ref, f32[4096]{0:T(1024)S(1)} %reshape.110.outof_ref, f32[2,16,8,128]{3,2,1,0:T(8,128)S(1)} %fusion.6.enter_ref), custom_call_target="tpu_custom_call" | custom-call | tf_op jit(solution)/shard_map/pallas_call | solution.py:465
  45.4 15.8 %shard_map.148 = bf16[1024,1024]{1,0:T(8,128)(2,1)S(1)} custom-call(bf16[256,1024]{1,0:T(8,128)(2,1)S(1)} %fusion.3.x_ref), custom_call_target="tpu_custom_call" | custom-call | tf_op jit(solution)/shard_map/pallas_call | solution.py:164
  61.3 1.3 copy-done.4
  63.6 5.2 %convolution_convert_fusion.x_ref = bf16[1024,1024]{1,0:T(8,128)(2,1)} fusion(bf16[1024,1024]{1,0:T(8,128)(2,1)} %copy-done.4, bf16[1024,1024]{1,0:T(8,128)(2,1)S(1)} %copy-done), kind=kOutput, calls=%fused_computation | convolution fusion | flops 2148532224 | bytes 6291456 | tf_op jit(solution)/shard_map/dot_general | solution.py:479
  68.9 1.6 copy-done.5
  70.5 31.1 %shard_map.149 = f32[256,512]{1,0:T(8,128)S(1)} custom-call(bf16[1024,1024]{1,0:T(8,128)(2,1)S(1)} %copy-done.5), custom_call_target="tpu_custom_call" | custom-call | tf_op jit(solution)/shard_map/pallas_call | solution.py:164
  103.6 49.1 %shard_map.150.rows_ref = bf16[512,4096]{1,0:T(8,128)(2,1)S(1)} custom-call(bf16[8,128,512]{2,1,0:T(8,128)(2,1)S(1)} %bitcast.80), custom_call_target="tpu_custom_call" | custom-call | tf_op jit(solution)/shard_map/pallas_call | solution.py:164
  154.2 21.6 %shard_map.151.act_ref = bf16[512,1792]{1,0:T(8,128)(2,1)S(1)} custom-call(bf16[512,4096]{1,0:T(8,128)(2,1)S(1)} %shard_map.150.rows_ref, f32[1,4096]{1,0:T(1,128)S(1)} %bitcast.85, bf16[1,4096,1792]{2,1,0:T(8,128)(2,1)} %gate_ref.1, bf16[1,4096,1792]{2,1,0:T(8,128)(2,1)} %up_ref.1), custom_call_target="tpu_custom_call" | custom-call | tf_op jit(solution)/shard_map/pallas_call | solution.py:98
  175.8 11.9 %shard_map.152 = bf16[512,4096]{1,0:T(8,128)(2,1)S(1)} custom-call(bf16[512,1792]{1,0:T(8,128)(2,1)S(1)} %shard_map.151.act_ref, bf16[1,1792,4096]{2,1,0:T(8,128)(2,1)} %weight_ref.1), custom_call_target="tpu_custom_call" | custom-call | tf_op jit(solution)/shard_map/pallas_call | solution.py:123
  187.8 32.4 %shard_map.153 = bf16[8,128,512]{2,1,0:T(8,128)(2,1)S(1)} custom-call(bf16[4,128,4096]{2,1,0:T(8,128)(2,1)S(1)} %bitcast.79, f32[128,512]{1,0:T(8,128)S(1)} %broadcast_in_dim.48.w_ref), custom_call_target="tpu_custom_call" | custom-call | tf_op jit(solution)/shard_map/pallas_call | solution.py:164
  (74 shorter events, 11.6 us)
Async XLA Ops:
  0.0 63.6 %copy-start = (bf16[1024,1024]{1,0:T(8,128)(2,1)S(1)}, bf16[1024,1024]{1,0:T(8,128)(2,1)}, u32[]{:S(2)}) copy-start(bf16[1024,1024]{1,0:T(8,128)(2,1)} %param.22) | copy-start | bytes 6291460
  0.0 10.0 %copy-start.10 = (f32[16,1024]{1,0:T(8,128)S(1)}, f32[16,1024]{1,0:T(8,128)}, u32[]{:S(2)}) copy-start(f32[16,1024]{1,0:T(8,128)} %param.18) | copy-start | bytes 196612
  1.9 8.2 %copy-start.12 = (f32[128,2,16]{0,2,1:T(8,128)S(1)}, f32[128,2,16]{0,2,1:T(8,128)}, u32[]{:S(2)}) copy-start(f32[128,2,16]{0,2,1:T(8,128)} %param.19) | copy-start | bytes 49156
  1.9 100.2 %collective-permute-start = (bf16[256,512]{1,0:T(8,128)(2,1)}, bf16[256,512]{1,0:T(8,128)(2,1)}, u32[]{:S(2)}, u32[]{:S(2)}) collective-permute-start(bf16[256,512]{1,0:T(8,128)(2,1)} %reshape.109), channel_id=1, source_target_pairs={{0,0},{1,1},{2,8},{3,9},{4,16},{5,17},{6,24},{7,25},{8,2},{9,3},{1... | collective-permute-start | bytes 786440 | tf_op jit(solution)/shard_map/ppermute | solution.py:432
  5.6 4.7 %copy-start.11 = (s32[128,2,2]{0,2,1:T(2,128)S(1)}, s32[128,2,2]{0,2,1:T(2,128)}, u32[]{:S(2)}) copy-start(s32[128,2,2]{0,2,1:T(2,128)} %param.28) | copy-start | bytes 6148
  10.8 1.2 copy-start.2
  24.9 8.0 %copy-start.13 = (f32[128,2,16]{0,2,1:T(8,128)S(1)}, f32[128,2,16]{0,2,1:T(8,128)}, u32[]{:S(2)}) copy-start(f32[128,2,16]{0,2,1:T(8,128)} %param.20) | copy-start | bytes 49156
  36.1 8.7 %copy-start.14 = (f32[1024]{0:T(1024)S(1)}, f32[1024]{0:T(1024)}, u32[]{:S(2)}) copy-start(f32[1024]{0:T(1024)} %param.21) | copy-start | bytes 12292
  37.2 1.2 copy-start.3
  38.5 6.4 %copy-start.7 = (f32[256,1024]{1,0:T(8,128)S(1)}, f32[256,1024]{1,0:T(8,128)}, u32[]{:S(2)}) copy-start(f32[256,1024]{1,0:T(8,128)} %reshape.113) | copy-start | bytes 3145732
  38.5 6.4 %copy-start.8 = (f32[256,1024]{1,0:T(8,128)S(1)}, f32[256,1024]{1,0:T(8,128)}, u32[]{:S(2)}) copy-start(f32[256,1024]{1,0:T(8,128)} %reshape.123) | copy-start | bytes 3145732
  45.4 17.2 %copy-start.9 = (s32[128,2,2]{1,0,2:T(8,128)S(1)}, s32[128,2,2]{1,0,2:T(8,128)}, u32[]{:S(2)}) copy-start(s32[128,2,2]{1,0,2:T(8,128)} %copy.44) | copy-start | bytes 6148
  45.4 18.2 %copy-start.15 = (f32[128,2,2]{0,2,1:T(2,128)S(1)}, f32[128,2,2]{0,2,1:T(2,128)}, u32[]{:S(2)}) copy-start(f32[128,2,2]{0,2,1:T(2,128)} %param.29) | copy-start | bytes 6148
  61.3 1.4 copy-start.4
  68.9 1.6 copy-start.5
  103.6 50.5 %copy-start.6 = (f32[4096]{0:T(1024)S(1)}, f32[4096]{0:T(1024)}, u32[]{:S(2)}) copy-start(f32[4096]{0:T(1024)} %param.24) | copy-start | bytes 49156
  152.7 67.5 %collective-permute-start.1 = (f32[256,512]{1,0:T(8,128)S(1)}, f32[256,512]{1,0:T(8,128)S(1)}, u32[]{:S(2)}, u32[]{:S(2)}) collective-permute-start(f32[256,512]{1,0:T(8,128)S(1)} %convert_add_fusion), channel_id=1, source_target_pairs={{0,0},{1,1},{2,8},{3,9},{4,16},{5,17},{6,24},{7,25},{8,2},{9,3},{1... | collective-permute-start | bytes 1572872 | tf_op jit(solution)/shard_map/ppermute | solution.py:491
  187.8 33.7 %copy-start.1 = (bf16[1024,1024]{1,0:T(8,128)(2,1)S(1)}, bf16[1024,1024]{1,0:T(8,128)(2,1)}, u32[]{:S(2)}) copy-start(bf16[1024,1024]{1,0:T(8,128)(2,1)} %param.22) | copy-start | bytes 6291460
